TPU v7x, 128 devices: a whole 4x4x4 slice. The times are simulated.
128 devices in a mesh: tm: 8 (over y_lo, z), space: 16 (over y_hi, x, core).
Axes of the slice: x: 4, y: 4 (y_hi: 2, y_lo: 2; y = y_hi * 2 + y_lo), z: 4, core: 2. Of those that a mesh axis runs over, the one named last changes fastest.
Arguments:
- probes: bfloat16 [384, 256, 1024], P('tm', 'space'), may hold values from -6 to 6
- local_links: int32 [256, 4], P('space'), may hold values from 0 to 15
- remote_links: int32 [256, 2], P('space'), may hold values from 0 to 31
- shared_blocks: int32 [16, 2], P('space'), may hold values from 0 to 15, as said below
- slab_days: int32 [8], P('tm'), may hold values from 1 to 48, 216 in all
- local_coupling: bfloat16 [256, 4, 64, 64], P('space'), may hold values from -0.3125 to 0.3125
- remote_coupling: bfloat16 [256, 2, 64, 64], P('space'), may hold values from -0.3125 to 0.3125
- block_inverse: bfloat16 [256, 64, 64], P('space'), may hold values from -0.0390625 to 0.0390625
- retention: float32 [384, 16384], P('tm', 'space'), as said below
Outputs:
- variance: float32 [384, 16384], P('tm', 'space')
Inputs may be any that keep to these rules, and one draw needn't show every extreme that they name: `shared_blocks`: each group's 2 numbers differ, and each list holds the group's last local block. `retention`: share of a node's state carried from one day to the next.
All inputs are finite; a program needn't handle non-finite values. No bound on the sum of `slab_days` on one device may be relied on, other than what follows from the above.
Results may differ from a plain program's by a relative error of at most 0.0028.
Values may be sent and summed in bfloat16 or wider, within the bound.
A program may use at most 192 MiB of HBM per device.

v0:
```python
import functools

import jax
import jax.numpy as jnp
from jax import lax
from jax.experimental import pallas as pl
from jax.experimental.pallas import tpu as pltpu
from jax.sharding import PartitionSpec as P

F32, BF16 = jnp.float32, jnp.bfloat16
MESH = pl.DeviceIdType.MESH
DAYS, BLOCKS, BS, PROBES, GROUPS, SLABS = 48, 16, 64, 16, 16, 8
WIDTH = BLOCKS * BS
ROWS = DAYS * PROBES
CHUNKS = 2
CHUNK_ROWS = ROWS // CHUNKS
CHUNK_DAYS = DAYS // CHUNKS
HALF = CHUNK_ROWS // 2
SUB = 192


def day_rows(t):
    return pl.ds(pl.multiple_of(t * PROBES, PROBES), PROBES)


def kernel(
    local_links,
    remote_links,
    shared_blocks,
    slab_days,
    probes_hbm,
    local_hbm,
    remote_hbm,
    inverse_hbm,
    retention_ref,
    out_ref,
    probes,
    local_w,
    remote_w,
    inverse_w,
    shuffle,
    shuffled,
    ordered,
    shared,
    near,
    far,
    forth,
    back,
    total,
    states,
    stored,
    retain,
    active,
    forward_decay,
    backward_decay,
    partial,
    slab_decay,
    ends,
    leaving,
    in_sem,
    send_sem,
    recv_sem,
    tm_send,
    tm_recv,
):
    tm = lax.axis_index("tm")
    space = lax.axis_index("space")
    core, x, y = space % 2, (space // 2) % 4, space // 8

    def at(dx, dy, dc):
        return ((y + dy) % 2 * 4 + (x + dx) % 4) * 2 + (core + dc) % 2

    me = at(0, 0, 0)
    sibling = at(0, 0, 1)

    barrier = pltpu.get_barrier_semaphore()
    for to in (at(1, 0, 0), at(3, 0, 0), at(0, 1, 0), sibling):
        pl.semaphore_signal(barrier, inc=1, device_id=(tm, to), device_id_type=MESH)
    for d in range(1, SLABS):
        pl.semaphore_signal(
            barrier, inc=1, device_id=((tm + d) % SLABS, space), device_id_type=MESH
        )

    fetch = []
    for k in range(CHUNKS):
        rows = pl.ds(k * CHUNK_ROWS, CHUNK_ROWS)
        fetch.append(pltpu.make_async_copy(probes_hbm.at[rows], probes.at[rows], in_sem.at[k]))
    weights = [
        pltpu.make_async_copy(local_hbm, local_w, in_sem.at[CHUNKS]),
        pltpu.make_async_copy(remote_hbm, remote_w, in_sem.at[CHUNKS + 1]),
        pltpu.make_async_copy(inverse_hbm, inverse_w, in_sem.at[CHUNKS + 2]),
    ]
    for copy in fetch + weights:
        copy.start()

    def shuffle_rows(r, carry):
        source = lax.broadcasted_iota(jnp.int32, (64, WIDTH), 0) + r * 64
        target = lax.broadcasted_iota(jnp.int32, (64, WIDTH), 1)
        hit = target == (source % PROBES) * BS + source // PROBES
        shuffle[pl.ds(pl.multiple_of(r * 64, 64), 64), :] = jnp.where(hit, 1.0, 0.0).astype(BF16)
        return carry

    lax.fori_loop(0, WIDTH // 64, shuffle_rows, 0)

    low = lax.broadcasted_iota(jnp.int32, (8, 128), 1) < BS

    def pair_up(first, second):
        mixed = pltpu.roll(jnp.where(low, second, first), BS, 1)
        return jnp.concatenate(
            [jnp.where(low, first, mixed), jnp.where(low, mixed, second)], axis=0
        ).astype(BF16)

    def block_row(t, b):
        return shuffled[pl.ds(pl.multiple_of((t * BLOCKS + b) * 8, 8), 8), :]

    def permute(k):
        def part(r, carry):
            lo = k * CHUNK_ROWS + r * SUB
            for n in range(4):
                value = jnp.dot(
                    probes[pl.ds(pl.multiple_of(lo, SUB), SUB), :],
                    shuffle[:, n * 256 : (n + 1) * 256],
                    preferred_element_type=F32,
                )
                for h in range(2):
                    shuffled[pl.ds(lo * 8 + 2 * n + h, SUB, stride=8), :] = value[
                        :, h * 128 : (h + 1) * 128
                    ]
            return carry

        lax.fori_loop(0, CHUNK_ROWS // SUB, part, 0)

    def pick_shared(k):
        b0, b1 = shared_blocks[0, 0], shared_blocks[0, 1]

        def day(t, carry):
            first = second = block_row(t + k * CHUNK_DAYS, 0)
            for b in range(1, BLOCKS):
                tile = block_row(t + k * CHUNK_DAYS, b)
                first = jnp.where(b0 == b, tile, first)
                second = jnp.where(b1 == b, tile, second)
            shared[k, me, day_rows(t), :] = pair_up(first, second)
            return carry

        lax.fori_loop(0, CHUNK_DAYS, day, 0)

    def order(k):
        def day(t, carry):
            for pair in range(BLOCKS // 2):
                ordered[day_rows(t), pair * 128 : (pair + 1) * 128] = pair_up(
                    block_row(t, 2 * pair), block_row(t, 2 * pair + 1)
                )
            return carry

        lax.fori_loop(k * CHUNK_DAYS, (k + 1) * CHUNK_DAYS, day, 0)

    used = [0]
    pending = []

    def send(slot, k, lo, rows, to):
        i = used[0]
        used[0] += 1
        where = shared.at[k, slot, pl.ds(lo, rows)]
        copy = pltpu.make_async_remote_copy(
            src_ref=where,
            dst_ref=where,
            send_sem=send_sem.at[i],
            recv_sem=recv_sem.at[i],
            device_id=(tm, to),
            device_id_type=MESH,
        )
        copy.start()
        pending.append(copy)
        return copy

    flows = [{} for _ in range(CHUNKS)]
    across = [[] for _ in range(CHUNKS)]
    N = CHUNK_ROWS

    def send_own(k):
        f = flows[k]
        f["y"] = send(me, k, 0, N, at(0, 1, 0))
        f["p0"] = send(me, k, 0, N, at(1, 0, 0))
        f["m0"] = send(me, k, 0, N, at(3, 0, 0))
        across[k].append(send(me, k, 0, N, sibling))

    def relay_first(k):
        f = flows[k]
        f["y"].wait_recv()
        f["p1"] = send(at(0, 1, 0), k, 0, N, at(1, 0, 0))
        f["m1"] = send(at(0, 1, 0), k, 0, N, at(3, 0, 0))
        across[k].append(send(at(0, 1, 0), k, 0, N, sibling))
        f["p0"].wait_recv()
        f["pp0"] = send(at(3, 0, 0), k, 0, HALF, at(1, 0, 0))
        across[k].append(send(at(3, 0, 0), k, 0, N, sibling))
        f["m0"].wait_recv()
        f["mm0"] = send(at(1, 0, 0), k, HALF, HALF, at(3, 0, 0))
        across[k].append(send(at(1, 0, 0), k, 0, N, sibling))

    def relay_second(k):
        f = flows[k]
        f["p1"].wait_recv()
        f["pp1"] = send(at(3, 1, 0), k, 0, HALF, at(1, 0, 0))
        across[k].append(send(at(3, 1, 0), k, 0, N, sibling))
        f["m1"].wait_recv()
        f["mm1"] = send(at(1, 1, 0), k, HALF, HALF, at(3, 0, 0))
        across[k].append(send(at(1, 1, 0), k, 0, N, sibling))

    def relay_third(k):
        f = flows[k]
        f["pp0"].wait_recv()
        f["mm0"].wait_recv()
        across[k].append(send(at(2, 0, 0), k, 0, N, sibling))
        f["pp1"].wait_recv()
        f["mm1"].wait_recv()
        across[k].append(send(at(2, 1, 0), k, 0, N, sibling))

    def all_here(k):
        for copy in across[k]:
            copy.wait_recv()

    def build(weight, links, count, degree, out):
        def pair_of(pair, carry):
            tiles = [
                jnp.transpose(
                    jnp.concatenate(
                        [weight[2 * pair, n].astype(F32), weight[2 * pair + 1, n].astype(F32)], axis=0
                    )
                )
                for n in range(degree)
            ]
            wanted = [
                jnp.where(low[0:1], links[2 * pair, n], links[2 * pair + 1, n])
                for n in range(degree)
            ]

            def source_block(r, c):
                value = tiles[0] * jnp.where(wanted[0] == r, 1.0, 0.0)
                for n in range(1, degree):
                    value = value + tiles[n] * jnp.where(wanted[n] == r, 1.0, 0.0)
                out[
                    pl.ds(pl.multiple_of(r * BS, BS), BS),
                    pl.ds(pl.multiple_of(pair * 128, 128), 128),
                ] = value.astype(BF16)
                return c

            return lax.fori_loop(0, count, source_block, carry)

        lax.fori_loop(0, BLOCKS // 2, pair_of, 0)

    def build_inverse():
        forth[...] = jnp.zeros_like(forth)
        back[...] = jnp.zeros_like(back)
        gap = jnp.zeros((BS, BS), F32)
        for b in range(BLOCKS):
            quad, place = b // 4, b % 4
            value = inverse_w[b].astype(F32)
            for out, tile in ((forth, jnp.transpose(value)), (back, value)):
                wide = jnp.concatenate([tile, gap] if place % 2 == 0 else [gap, tile], axis=1)
                lane = place // 2 * 128
                out[quad, place * BS : (place + 1) * BS, lane : lane + 128] = wide.astype(BF16)

    def couple_local(k):
        def part(r, carry):
            rows = pl.ds(pl.multiple_of(k * CHUNK_ROWS + r * SUB, SUB), SUB)
            for n in range(4):
                cols = slice(n * 256, (n + 1) * 256)
                total[rows, cols] = ordered[rows, cols].astype(F32) - jnp.dot(
                    ordered[rows, :], near[:, cols], preferred_element_type=F32
                )
            return carry

        lax.fori_loop(0, CHUNK_ROWS // SUB, part, 0)

    def couple_remote(k):
        def part(r, carry):
            rows = pl.ds(pl.multiple_of(k * CHUNK_ROWS + r * SUB, SUB), SUB)
            inner = pl.ds(pl.multiple_of(r * SUB, SUB), SUB)
            left = jnp.concatenate([shared[k, g, inner, :] for g in range(GROUPS)], axis=1)
            for n in range(4):
                cols = slice(n * 256, (n + 1) * 256)
                source = (
                    total[rows, cols] - jnp.dot(left, far[:, cols], preferred_element_type=F32)
                ).astype(BF16)
                states[rows, cols] = jnp.dot(source, forth[n], preferred_element_type=F32)
            return carry

        lax.fori_loop(0, CHUNK_ROWS // SUB, part, 0)

    def scan_forward(k, state):
        def day(t, s):
            s = s * retain[pl.ds(t, 1), :] + states[day_rows(t), :] * active[pl.ds(t, 1), :]
            states[day_rows(t), :] = s
            return s

        return lax.fori_loop(k * CHUNK_DAYS, (k + 1) * CHUNK_DAYS, day, state)

    def prepare_decay():
        on = lax.broadcasted_iota(jnp.int32, (DAYS, WIDTH), 0) < slab_days[0]
        active[...] = jnp.where(on, 1.0, 0.0)
        retain[0:DAYS, :] = jnp.where(on, retention_ref[...], 1.0)
        retain[DAYS : DAYS + 8, :] = jnp.ones((8, WIDTH), F32)

        def ahead(t, d):
            d = d * retain[pl.ds(t, 1), :]
            forward_decay[pl.ds(t, 1), :] = d
            return d

        product = lax.fori_loop(0, DAYS, ahead, jnp.ones((1, WIDTH), F32))

        def behind(i, d):
            t = DAYS - 1 - i
            d = d * retain[pl.ds(t + 1, 1), :]
            backward_decay[pl.ds(t, 1), :] = d
            return d

        lax.fori_loop(0, DAYS, behind, jnp.ones((1, WIDTH), F32))
        for q in range(8):
            slab_decay[tm, q : q + 1, :] = product[:, q * 128 : (q + 1) * 128]

    def tm_copy(buf, kind, d):
        to = (tm + d) % SLABS if kind < 2 else (tm + SLABS - d) % SLABS
        return pltpu.make_async_remote_copy(
            src_ref=buf.at[tm],
            dst_ref=buf.at[tm],
            send_sem=tm_send.at[kind * 8 + d],
            recv_sem=tm_recv.at[kind * 8 + d],
            device_id=(to, space),
            device_id_type=MESH,
        )

    def decay_of(s):
        return jnp.concatenate([slab_decay[s, q : q + 1, :] for q in range(8)], axis=1)

    for k in range(CHUNKS):
        fetch[k].wait()
        permute(k)
        pick_shared(k)
    pl.semaphore_wait(barrier, 4 + SLABS - 1)
    for k in range(CHUNKS):
        send_own(k)
    prepare_decay()
    decay_copies = [tm_copy(slab_decay, 0, d) for d in range(1, SLABS)]
    for copy in decay_copies:
        copy.start()
    order(0)
    relay_first(0)
    order(1)
    relay_first(1)
    weights[0].wait()
    build(local_w, local_links, BLOCKS, 4, near)
    relay_second(0)
    weights[1].wait()
    build(remote_w, remote_links, 2 * GROUPS, 2, far)
    relay_second(1)
    couple_local(0)
    relay_third(0)
    couple_local(1)
    weights[2].wait()
    build_inverse()
    all_here(0)
    couple_remote(0)
    state = scan_forward(0, jnp.zeros((PROBES, WIDTH), F32))
    relay_third(1)
    all_here(1)
    couple_remote(1)
    state = scan_forward(1, state)
    ends[tm] = state
    for d in range(1, SLABS):

        @pl.when(tm + d < SLABS)
        def _():
            tm_copy(ends, 1, d).start()

    for copy in decay_copies:
        copy.wait_recv()
    for d in range(1, SLABS):

        @pl.when(tm - d >= 0)
        def _():
            tm_copy(ends, 1, d).wait_recv()

    carry = jnp.zeros((PROBES, WIDTH), F32)
    for s in range(SLABS - 1):
        carry = jnp.where(s < tm, decay_of(s) * carry + ends[s], carry)

    leave = jnp.zeros((PROBES, WIDTH), F32)
    for k in reversed(range(CHUNKS)):

        def fix(t, c):
            stored[day_rows(t), :] = (
                states[day_rows(t), :] + forward_decay[pl.ds(t, 1), :] * c
            ).astype(BF16)
            return c

        carry = lax.fori_loop(k * CHUNK_DAYS, (k + 1) * CHUNK_DAYS, fix, carry)

        def part(r, c):
            rows = pl.ds(pl.multiple_of(k * CHUNK_ROWS + r * SUB, SUB), SUB)
            for n in range(4):
                cols = slice(n * 256, (n + 1) * 256)
                total[rows, cols] = jnp.dot(stored[rows, cols], back[n], preferred_element_type=F32)
            return c

        lax.fori_loop(0, CHUNK_ROWS // SUB, part, 0)

        def day(i, u):
            t = (k + 1) * CHUNK_DAYS - 1 - i
            u = total[day_rows(t), :] * active[pl.ds(t, 1), :] + retain[pl.ds(t + 1, 1), :] * u
            partial[pl.ds(t, 1), :] = jnp.sum(
                ordered[day_rows(t), :].astype(F32) * u, axis=0, keepdims=True
            )
            return u

        leave = lax.fori_loop(0, CHUNK_DAYS, day, leave)
    leaving[tm] = leave * retain[0:1, :]
    for d in range(1, SLABS):

        @pl.when(tm - d >= 0)
        def _():
            tm_copy(leaving, 2, d).start()

    for copy in pending:
        copy.wait_send()
    for copy in decay_copies:
        copy.wait_send()
    for d in range(1, SLABS):

        @pl.when(tm + d < SLABS)
        def _():
            tm_copy(ends, 1, d).wait_send()
            tm_copy(leaving, 2, d).wait_recv()

    carry = jnp.zeros((PROBES, WIDTH), F32)
    for s in reversed(range(1, SLABS)):
        carry = jnp.where(s > tm, decay_of(s) * carry + leaving[s], carry)

    def finish(t, c):
        extra = jnp.sum(ordered[day_rows(t), :].astype(F32) * c, axis=0, keepdims=True)
        out_ref[pl.ds(t, 1), :] = (
            partial[pl.ds(t, 1), :] + backward_decay[pl.ds(t, 1), :] * extra
        ) * (1.0 / PROBES)
        return c

    lax.fori_loop(0, DAYS, finish, carry)
    for d in range(1, SLABS):

        @pl.when(tm - d >= 0)
        def _():
            tm_copy(leaving, 2, d).wait_send()


def local(
    probes,
    local_links,
    remote_links,
    shared_blocks,
    slab_days,
    local_coupling,
    remote_coupling,
    block_inverse,
    retention,
):
    smem = pl.BlockSpec(memory_space=pltpu.SMEM)
    vmem = pl.BlockSpec(memory_space=pltpu.VMEM)
    anywhere = pl.BlockSpec(memory_space=pl.ANY)
    return pl.pallas_call(
        kernel,
        out_shape=jax.ShapeDtypeStruct((DAYS, WIDTH), F32),
        in_specs=[smem] * 4 + [anywhere] * 4 + [vmem],
        out_specs=vmem,
        scratch_shapes=[
            pltpu.VMEM((ROWS, WIDTH), BF16),
            pltpu.VMEM(local_coupling.shape, BF16),
            pltpu.VMEM(remote_coupling.shape, BF16),
            pltpu.VMEM(block_inverse.shape, BF16),
            pltpu.VMEM((WIDTH, WIDTH), BF16),
            pltpu.VMEM((ROWS * 8, 128), F32),
            pltpu.VMEM((ROWS, WIDTH), BF16),
            pltpu.VMEM((CHUNKS, GROUPS, CHUNK_ROWS, 128), BF16),
            pltpu.VMEM((WIDTH, WIDTH), BF16),
            pltpu.VMEM((2 * WIDTH, WIDTH), BF16),
            pltpu.VMEM((4, 256, 256), BF16),
            pltpu.VMEM((4, 256, 256), BF16),
            pltpu.VMEM((ROWS, WIDTH), F32),
            pltpu.VMEM((ROWS, WIDTH), F32),
            pltpu.VMEM((ROWS, WIDTH), BF16),
            pltpu.VMEM((DAYS + 8, WIDTH), F32),
            pltpu.VMEM((DAYS, WIDTH), F32),
            pltpu.VMEM((DAYS, WIDTH), F32),
            pltpu.VMEM((DAYS, WIDTH), F32),
            pltpu.VMEM((DAYS, WIDTH), F32),
            pltpu.VMEM((SLABS, 8, 128), F32),
            pltpu.VMEM((SLABS, PROBES, WIDTH), F32),
            pltpu.VMEM((SLABS, PROBES, WIDTH), F32),
            pltpu.SemaphoreType.DMA((CHUNKS + 3,)),
            pltpu.SemaphoreType.DMA((CHUNKS * 20,)),
            pltpu.SemaphoreType.DMA((CHUNKS * 20,)),
            pltpu.SemaphoreType.DMA((24,)),
            pltpu.SemaphoreType.DMA((24,)),
        ],
        compiler_params=pltpu.CompilerParams(
            vmem_limit_bytes=60 << 20, collective_id=0, has_side_effects=True
        ),
    )(
        local_links,
        remote_links,
        shared_blocks,
        slab_days,
        probes.reshape(ROWS, WIDTH),
        local_coupling,
        remote_coupling,
        block_inverse,
        retention,
    )


def solution(mesh):
    placed = (
        P("tm", "space", None),
        P("space", None),
        P("space", None),
        P("space", None),
        P("tm"),
        P("space", None, None, None),
        P("space", None, None, None),
        P("space", None, None),
        P("tm", "space"),
    )
    return jax.shard_map(
        local, mesh=mesh, in_specs=placed, out_specs=P("tm", "space"), check_vma=False
    )
```

profile of v0, /device:TPU:0, one launch (start us, length us, event | category | flops | bytes accessed | tf_op | source)
XLA Modules:
  0.0 70.6 jit_solution(10111988996174058712)
XLA Ops:
  0.7 1.4 %copy.10.local_links = s32[16,4]{1,0:T(8,128)} copy(s32[16,4]{0,1:T(4,128)} %param.10) | data formatting | bytes 512 | tf_op args[1]
  2.0 1.3 %copy.11.remote_links = s32[16,2]{1,0:T(8,128)} copy(s32[16,2]{0,1:T(2,128)} %param.11) | data formatting | bytes 256 | tf_op args[2]
  3.4 65.7 %shard_map.91 = f32[48,1024]{1,0:T(8,128)} custom-call(s32[16,4]{1,0:T(8,128)} %copy.10.local_links, s32[16,2]{1,0:T(8,128)} %copy.11.remote_links, s32[1,2]{1,0:T(1,128)} %shared_blocks.1, s32[1]{0:T(128)S(6)} %copy.13.slab_days, bf16[768,1024]{1,0:T(8,128)(2,1)} %bitcast.1, bf16[16,4,64,64]{3,2,1,0:T(8,128)(2,1)} %local_hbm.1, ...), custom_call_target="tpu_custom_call" | custom-call | tf_op jit(solution)/shard_map/pallas_call | solution.py:467
  69.0 1.6 %copy.14 = f32[48,1024]{1,0:T(8,128)} copy(f32[48,1024]{1,0:T(8,128)} %shard_map.91) | data formatting | bytes 393216
where the time goes:
time: 70.9 us; the launch traced here: 70.6 us
  Pallas kernels  65.7 us (93%)
  local copies, waits for them, and re-layouts  4.32 us (6%)
    pallas_call x1, Pallas kernels, local(): pl.pallas_call(kernel, out_shape=jax.ShapeDtypeStruct((DAYS, WIDTH), F32)...  65.7 us
    unnamed x3, local copies, waits for them, and re-layouts  4.32 us

commit v1 on v0

--- a/solution.py
+++ b/solution.py
@@ -40,8 +40,11 @@
     inverse_w,
     shuffle,
     shuffled,
+    picked,
+    picked_shuffled,
     ordered,
     shared,
+    tiles,
     near,
     far,
     forth,
@@ -108,7 +111,7 @@
         mixed = pltpu.roll(jnp.where(low, second, first), BS, 1)
         return jnp.concatenate(
             [jnp.where(low, first, mixed), jnp.where(low, mixed, second)], axis=0
-        ).astype(BF16)
+        )
 
     def block_row(t, b):
         return shuffled[pl.ds(pl.multiple_of((t * BLOCKS + b) * 8, 8), 8), :]
@@ -130,29 +133,50 @@
 
         lax.fori_loop(0, CHUNK_ROWS // SUB, part, 0)
 
-    def pick_shared(k):
-        b0, b1 = shared_blocks[0, 0], shared_blocks[0, 1]
-
-        def day(t, carry):
-            first = second = block_row(t + k * CHUNK_DAYS, 0)
-            for b in range(1, BLOCKS):
-                tile = block_row(t + k * CHUNK_DAYS, b)
-                first = jnp.where(b0 == b, tile, first)
-                second = jnp.where(b1 == b, tile, second)
-            shared[k, me, day_rows(t), :] = pair_up(first, second)
+    def pick_shared():
+        row = lax.broadcasted_iota(jnp.int32, (2 * DAYS, ROWS), 0)
+        column = lax.broadcasted_iota(jnp.int32, (2 * DAYS, ROWS), 1)
+        second = row >= DAYS
+        day = jnp.where(second, row - DAYS, row)
+        wanted = day * BLOCKS + jnp.where(second, shared_blocks[0, 1], shared_blocks[0, 0])
+        select = jnp.where(column == wanted, 1.0, 0.0).astype(BF16)
+        for n in range(4):
+            cols = slice(n * 256, (n + 1) * 256)
+            picked[:, cols] = jnp.dot(
+                select, probes[:, cols], preferred_element_type=F32
+            ).astype(BF16)
+        for n in range(4):
+            value = jnp.dot(
+                picked[...], shuffle[:, n * 256 : (n + 1) * 256], preferred_element_type=F32
+            )
+            for h in range(2):
+                picked_shuffled[pl.ds(2 * n + h, 2 * DAYS, stride=8), :] = value[
+                    :, h * 128 : (h + 1) * 128
+                ]
+
+        def days(g, carry):
+            for i in range(4):
+                t = g * 4 + i
+                tiles = [
+                    picked_shuffled[pl.ds(pl.multiple_of((m * DAYS + t) * 8, 8), 8), :]
+                    for m in range(2)
+                ]
+                shared[t // CHUNK_DAYS, me, day_rows(t % CHUNK_DAYS), :] = pair_up(*tiles).astype(BF16)
             return carry
 
-        lax.fori_loop(0, CHUNK_DAYS, day, 0)
+        lax.fori_loop(0, DAYS // 4, days, 0)
 
     def order(k):
-        def day(t, carry):
-            for pair in range(BLOCKS // 2):
-                ordered[day_rows(t), pair * 128 : (pair + 1) * 128] = pair_up(
-                    block_row(t, 2 * pair), block_row(t, 2 * pair + 1)
-                )
+        def days(g, carry):
+            for i in range(4):
+                t = g * 4 + i
+                for pair in range(BLOCKS // 2):
+                    value = pair_up(block_row(t, 2 * pair), block_row(t, 2 * pair + 1))
+                    total[day_rows(t), pair * 128 : (pair + 1) * 128] = value
+                    ordered[day_rows(t), pair * 128 : (pair + 1) * 128] = value.astype(BF16)
             return carry
 
-        lax.fori_loop(k * CHUNK_DAYS, (k + 1) * CHUNK_DAYS, day, 0)
+        lax.fori_loop(k * CHUNK_DAYS // 4, (k + 1) * CHUNK_DAYS // 4, days, 0)
 
     used = [0]
     pending = []
@@ -219,32 +243,36 @@
         for copy in across[k]:
             copy.wait_recv()
 
-    def build(weight, links, count, degree, out):
-        def pair_of(pair, carry):
-            tiles = [
-                jnp.transpose(
+    def turn(weight, degree, first):
+        for pair in range(BLOCKS // 2):
+            for n in range(degree):
+                tiles[pair, first + n] = jnp.transpose(
                     jnp.concatenate(
                         [weight[2 * pair, n].astype(F32), weight[2 * pair + 1, n].astype(F32)], axis=0
                     )
-                )
+                ).astype(BF16)
+
+    def build(links, count, degree, first, out):
+        def pair_of(pair, carry):
+            parts = [tiles[pair, first + n] for n in range(degree)]
+            wanted = [
+                jnp.where(low[0:1], links[n, 2 * pair], links[n, 2 * pair + 1])
                 for n in range(degree)
             ]
-            wanted = [
-                jnp.where(low[0:1], links[2 * pair, n], links[2 * pair + 1, n])
-                for n in range(degree)
-            ]
-
-            def source_block(r, c):
-                value = tiles[0] * jnp.where(wanted[0] == r, 1.0, 0.0)
-                for n in range(1, degree):
-                    value = value + tiles[n] * jnp.where(wanted[n] == r, 1.0, 0.0)
-                out[
-                    pl.ds(pl.multiple_of(r * BS, BS), BS),
-                    pl.ds(pl.multiple_of(pair * 128, 128), 128),
-                ] = value.astype(BF16)
+
+            def source_blocks(g, c):
+                for i in range(4):
+                    r = g * 4 + i
+                    terms = [
+                        p * jnp.where(w == r, 1.0, 0.0).astype(BF16) for p, w in zip(parts, wanted)
+                    ]
+                    out[
+                        pl.ds(pl.multiple_of(r * BS, BS), BS),
+                        pl.ds(pl.multiple_of(pair * 128, 128), 128),
+                    ] = functools.reduce(lambda u, v: u + v, terms)
                 return c
 
-            return lax.fori_loop(0, count, source_block, carry)
+            return lax.fori_loop(0, count // 4, source_blocks, carry)
 
         lax.fori_loop(0, BLOCKS // 2, pair_of, 0)
 
@@ -265,7 +293,7 @@
             rows = pl.ds(pl.multiple_of(k * CHUNK_ROWS + r * SUB, SUB), SUB)
             for n in range(4):
                 cols = slice(n * 256, (n + 1) * 256)
-                total[rows, cols] = ordered[rows, cols].astype(F32) - jnp.dot(
+                total[rows, cols] = total[rows, cols] - jnp.dot(
                     ordered[rows, :], near[:, cols], preferred_element_type=F32
                 )
             return carry
@@ -276,13 +304,17 @@
         def part(r, carry):
             rows = pl.ds(pl.multiple_of(k * CHUNK_ROWS + r * SUB, SUB), SUB)
             inner = pl.ds(pl.multiple_of(r * SUB, SUB), SUB)
-            left = jnp.concatenate([shared[k, g, inner, :] for g in range(GROUPS)], axis=1)
             for n in range(4):
                 cols = slice(n * 256, (n + 1) * 256)
-                source = (
-                    total[rows, cols] - jnp.dot(left, far[:, cols], preferred_element_type=F32)
-                ).astype(BF16)
-                states[rows, cols] = jnp.dot(source, forth[n], preferred_element_type=F32)
+                left = jnp.concatenate([shared[k, g, inner, :] for g in range(GROUPS)], axis=1)
+                total[rows, cols] = total[rows, cols] - jnp.dot(
+                    left, far[:, cols], preferred_element_type=F32
+                )
+            for n in range(4):
+                cols = slice(n * 256, (n + 1) * 256)
+                states[rows, cols] = jnp.dot(
+                    total[rows, cols].astype(BF16), forth[n], preferred_element_type=F32
+                )
             return carry
 
         lax.fori_loop(0, CHUNK_ROWS // SUB, part, 0)
@@ -334,24 +366,27 @@
 
     for k in range(CHUNKS):
         fetch[k].wait()
-        permute(k)
-        pick_shared(k)
+    pick_shared()
+    prepare_decay()
     pl.semaphore_wait(barrier, 4 + SLABS - 1)
     for k in range(CHUNKS):
         send_own(k)
-    prepare_decay()
     decay_copies = [tm_copy(slab_decay, 0, d) for d in range(1, SLABS)]
     for copy in decay_copies:
         copy.start()
+    permute(0)
+    permute(1)
+    relay_first(0)
     order(0)
-    relay_first(0)
+    relay_first(1)
     order(1)
-    relay_first(1)
     weights[0].wait()
-    build(local_w, local_links, BLOCKS, 4, near)
+    turn(local_w, 4, 0)
+    build(local_links, BLOCKS, 4, 0, near)
     relay_second(0)
     weights[1].wait()
-    build(remote_w, remote_links, 2 * GROUPS, 2, far)
+    turn(remote_w, 2, 4)
+    build(remote_links, 2 * GROUPS, 2, 4, far)
     relay_second(1)
     couple_local(0)
     relay_third(0)
@@ -384,36 +419,69 @@
     for s in range(SLABS - 1):
         carry = jnp.where(s < tm, decay_of(s) * carry + ends[s], carry)
 
-    leave = jnp.zeros((PROBES, WIDTH), F32)
-    for k in reversed(range(CHUNKS)):
-
-        def fix(t, c):
-            stored[day_rows(t), :] = (
-                states[day_rows(t), :] + forward_decay[pl.ds(t, 1), :] * c
-            ).astype(BF16)
+    row8 = lax.broadcasted_iota(jnp.int32, (8, 128), 0)
+
+    def fold(values):
+        for step in (1, 2, 4):
+            keep = (row8 & step) == 0
+            values = [
+                jnp.where(keep, u, v) + pltpu.roll(jnp.where(keep, v, u), step, 0)
+                for u, v in zip(values[0::2], values[1::2])
+            ]
+        return values[0]
+
+    def adjoint_sweep(carry, with_sums):
+        def fix(g, c):
+            for i in range(2):
+                t = 2 * g + i
+                stored[day_rows(t), :] = (
+                    states[day_rows(t), :] + forward_decay[pl.ds(t, 1), :] * c
+                ).astype(BF16)
             return c
 
-        carry = lax.fori_loop(k * CHUNK_DAYS, (k + 1) * CHUNK_DAYS, fix, carry)
+        lax.fori_loop(0, DAYS // 2, fix, carry)
 
         def part(r, c):
-            rows = pl.ds(pl.multiple_of(k * CHUNK_ROWS + r * SUB, SUB), SUB)
+            rows = pl.ds(pl.multiple_of(r * SUB, SUB), SUB)
             for n in range(4):
                 cols = slice(n * 256, (n + 1) * 256)
                 total[rows, cols] = jnp.dot(stored[rows, cols], back[n], preferred_element_type=F32)
             return c
 
-        lax.fori_loop(0, CHUNK_ROWS // SUB, part, 0)
-
-        def day(i, u):
-            t = (k + 1) * CHUNK_DAYS - 1 - i
-            u = total[day_rows(t), :] * active[pl.ds(t, 1), :] + retain[pl.ds(t + 1, 1), :] * u
-            partial[pl.ds(t, 1), :] = jnp.sum(
-                ordered[day_rows(t), :].astype(F32) * u, axis=0, keepdims=True
+        lax.fori_loop(0, ROWS // SUB, part, 0)
+        leave = []
+        for n in range(4):
+            cols = slice(n * 256, (n + 1) * 256)
+
+            def days(i, u):
+                g = DAYS // 8 - 1 - i
+                sums = [[None] * 8, [None] * 8]
+                for j in reversed(range(8)):
+                    t = g * 8 + j
+                    u = total[day_rows(t), cols] * active[pl.ds(t, 1), cols] + retain[
+                        pl.ds(t + 1, 1), cols
+                    ] * u
+                    if with_sums:
+                        product = ordered[day_rows(t), cols].astype(F32) * u
+                        for h in range(2):
+                            half = product[:, h * 128 : (h + 1) * 128]
+                            sums[h][j] = half[0:8] + half[8:16]
+                if with_sums:
+                    eight = pl.ds(pl.multiple_of(g * 8, 8), 8)
+                    for h in range(2):
+                        lane = n * 256 + h * 128
+                        partial[eight, lane : lane + 128] = fold(sums[h])
+                return u
+
+            leave.append(
+                lax.fori_loop(0, DAYS // 8, days, jnp.zeros((PROBES, 256), F32))
+                * retain[0:1, cols]
             )
-            return u
-
-        leave = lax.fori_loop(0, CHUNK_DAYS, day, leave)
-    leaving[tm] = leave * retain[0:1, :]
+        return leave
+
+    leave = adjoint_sweep(carry, True)
+    for n in range(4):
+        leaving[tm, :, n * 256 : (n + 1) * 256] = leave[n]
     for d in range(1, SLABS):
 
         @pl.when(tm - d >= 0)
@@ -435,14 +503,25 @@
     for s in reversed(range(1, SLABS)):
         carry = jnp.where(s > tm, decay_of(s) * carry + leaving[s], carry)
 
-    def finish(t, c):
-        extra = jnp.sum(ordered[day_rows(t), :].astype(F32) * c, axis=0, keepdims=True)
-        out_ref[pl.ds(t, 1), :] = (
-            partial[pl.ds(t, 1), :] + backward_decay[pl.ds(t, 1), :] * extra
-        ) * (1.0 / PROBES)
-        return c
-
-    lax.fori_loop(0, DAYS, finish, carry)
+    for n in range(8):
+        cols = slice(n * 128, (n + 1) * 128)
+        part_carry = carry[:, cols]
+
+        def finish(g, c):
+            eight = pl.ds(pl.multiple_of(g * 8, 8), 8)
+            z = ordered[pl.ds(pl.multiple_of(g * 128, 128), 128), cols].astype(F32)
+            extra = fold(
+                [
+                    z[16 * d : 16 * d + 8] * c[0:8] + z[16 * d + 8 : 16 * d + 16] * c[8:16]
+                    for d in range(8)
+                ]
+            )
+            out_ref[eight, cols] = (partial[eight, cols] + backward_decay[eight, cols] * extra) * (
+                1.0 / PROBES
+            )
+            return c
+
+        lax.fori_loop(0, DAYS // 8, finish, part_carry)
     for d in range(1, SLABS):
 
         @pl.when(tm - d >= 0)
@@ -476,8 +555,11 @@
             pltpu.VMEM(block_inverse.shape, BF16),
             pltpu.VMEM((WIDTH, WIDTH), BF16),
             pltpu.VMEM((ROWS * 8, 128), F32),
+            pltpu.VMEM((2 * DAYS, WIDTH), BF16),
+            pltpu.VMEM((2 * DAYS * 8, 128), F32),
             pltpu.VMEM((ROWS, WIDTH), BF16),
             pltpu.VMEM((CHUNKS, GROUPS, CHUNK_ROWS, 128), BF16),
+            pltpu.VMEM((BLOCKS // 2, 6, BS, 128), BF16),
             pltpu.VMEM((WIDTH, WIDTH), BF16),
             pltpu.VMEM((2 * WIDTH, WIDTH), BF16),
             pltpu.VMEM((4, 256, 256), BF16),
@@ -503,8 +585,8 @@
             vmem_limit_bytes=60 << 20, collective_id=0, has_side_effects=True
         ),
     )(
-        local_links,
-        remote_links,
+        local_links.T,
+        remote_links.T,
         shared_blocks,
         slab_days,
         probes.reshape(ROWS, WIDTH),

time: 70.9 us -> 58.2 us (0.82)
  Pallas kernels: 65.7 us -> 55.7 us
  local copies, waits for them, and re-layouts: 4.32 us -> 1.62 us
    pallas_call x1, Pallas kernels: 65.7 us -> 55.7 us  [local(): pl.pallas_call(kernel, out_shape=jax.ShapeDtypeStruct((DAYS, WIDTH), F32)...]
    unnamed x3 -> x1, local copies, waits for them, and re-layouts: 4.32 us -> 1.62 us
where the time goes in v1:
time: 58.2 us; the launch traced here: 58 us
  Pallas kernels  55.7 us (96%)
  local copies, waits for them, and re-layouts  1.62 us (3%)
  between operations  0.66 us (1%)
    pallas_call x1, Pallas kernels, local(): pl.pallas_call(kernel, out_shape=jax.ShapeDtypeStruct((DAYS, WIDTH), F32)...  55.7 us
    unnamed x1, local copies, waits for them, and re-layouts  1.62 us

profile of v1, /device:TPU:0, one launch (start us, length us, event | category | flops | bytes accessed | tf_op | source)
XLA Modules:
  0.0 58.0 jit_solution(4467078836844841637)
XLA Ops:
  0.7 55.7 %shard_map.91 = f32[48,1024]{1,0:T(8,128)} custom-call(s32[4,16]{1,0:T(4,128)} %bitcast.4, s32[2,16]{1,0:T(2,128)} %bitcast.5, s32[1,2]{1,0:T(1,128)} %shared_blocks.1, s32[1]{0:T(128)S(6)} %copy.11.slab_days, bf16[768,1024]{1,0:T(8,128)(2,1)} %bitcast.3, bf16[16,4,64,64]{3,2,1,0:T(8,128)(2,1)} %local_hbm.1, bf16[16,2,64,64]{3,2,1,0:T(8,128)(2,1)} %remote_hbm.1, ...), custom_call_target="tpu_custom_call" | custom-call | tf_op jit(solution)/shard_map/pallas_call | solution.py:546
  56.3 1.6 %copy.12 = f32[48,1024]{1,0:T(8,128)} copy(f32[48,1024]{1,0:T(8,128)} %shard_map.91) | data formatting | bytes 393216

commit v2 on v1

--- a/solution.py
+++ b/solution.py
@@ -58,8 +58,11 @@
     backward_decay,
     partial,
     slab_decay,
+    response,
     ends,
+    ends_short,
     leaving,
+    leaving_short,
     in_sem,
     send_sem,
     recv_sem,
@@ -360,6 +363,40 @@
             device_id=(to, space),
             device_id_type=MESH,
         )
+
+    def same_row(other):
+        return other // (SLABS // 2) == tm // (SLABS // 2)
+
+    def exchange(kind, wide, narrow, act):
+        for d in range(1, SLABS):
+            ahead = (kind == 1) == (act != "wait_recv")
+            other = tm + d if ahead else tm - d
+            real = other < SLABS if ahead else other >= 0
+            near_by = same_row(other)
+
+            @pl.when(jnp.logical_and(real, near_by))
+            def _():
+                getattr(tm_copy(wide, kind, d), act)()
+
+            @pl.when(jnp.logical_and(real, jnp.logical_not(near_by)))
+            def _():
+                getattr(tm_copy(narrow, kind, d), act)()
+
+    def arrived(s, wide, narrow):
+        return jnp.where(same_row(s), wide[s], narrow[s].astype(F32))
+
+    def prepare_response():
+        for n in range(4):
+            cols = slice(n * 256, (n + 1) * 256)
+            decay = forward_decay[:, cols]
+            gram = lax.dot_general(
+                decay * active[:, cols],
+                decay,
+                (((0,), (0,)), ((), ())),
+                precision=lax.Precision.HIGHEST,
+                preferred_element_type=F32,
+            )
+            response[n] = gram * back[n].astype(F32)
 
     def decay_of(s):
         return jnp.concatenate([slab_decay[s, q : q + 1, :] for q in range(8)], axis=1)
@@ -393,6 +430,7 @@
     couple_local(1)
     weights[2].wait()
     build_inverse()
+    prepare_response()
     all_here(0)
     couple_remote(0)
     state = scan_forward(0, jnp.zeros((PROBES, WIDTH), F32))
@@ -401,23 +439,8 @@
     couple_remote(1)
     state = scan_forward(1, state)
     ends[tm] = state
-    for d in range(1, SLABS):
-
-        @pl.when(tm + d < SLABS)
-        def _():
-            tm_copy(ends, 1, d).start()
-
-    for copy in decay_copies:
-        copy.wait_recv()
-    for d in range(1, SLABS):
-
-        @pl.when(tm - d >= 0)
-        def _():
-            tm_copy(ends, 1, d).wait_recv()
-
-    carry = jnp.zeros((PROBES, WIDTH), F32)
-    for s in range(SLABS - 1):
-        carry = jnp.where(s < tm, decay_of(s) * carry + ends[s], carry)
+    ends_short[tm] = state.astype(BF16)
+    exchange(1, ends, ends_short, "start")
 
     row8 = lax.broadcasted_iota(jnp.int32, (8, 128), 0)
 
@@ -434,9 +457,10 @@
         def fix(g, c):
             for i in range(2):
                 t = 2 * g + i
-                stored[day_rows(t), :] = (
-                    states[day_rows(t), :] + forward_decay[pl.ds(t, 1), :] * c
-                ).astype(BF16)
+                value = states[day_rows(t), :]
+                if with_sums:
+                    value = value + forward_decay[pl.ds(t, 1), :] * c
+                stored[day_rows(t), :] = value.astype(BF16)
             return c
 
         lax.fori_loop(0, DAYS // 2, fix, carry)
@@ -479,29 +503,36 @@
             )
         return leave
 
-    leave = adjoint_sweep(carry, True)
+    leave = adjoint_sweep(0, False)
+    for copy in decay_copies:
+        copy.wait_recv()
+    exchange(1, ends, ends_short, "wait_recv")
+    carry = jnp.zeros((PROBES, WIDTH), F32)
+    for s in range(SLABS - 1):
+        carry = jnp.where(s < tm, decay_of(s) * carry + arrived(s, ends, ends_short), carry)
     for n in range(4):
-        leaving[tm, :, n * 256 : (n + 1) * 256] = leave[n]
-    for d in range(1, SLABS):
-
-        @pl.when(tm - d >= 0)
-        def _():
-            tm_copy(leaving, 2, d).start()
+        cols = slice(n * 256, (n + 1) * 256)
+        value = leave[n] + jnp.dot(
+            carry[:, cols],
+            response[n],
+            precision=lax.Precision.HIGHEST,
+            preferred_element_type=F32,
+        )
+        leaving[tm, :, cols] = value
+        leaving_short[tm, :, cols] = value.astype(BF16)
+    exchange(2, leaving, leaving_short, "start")
+    adjoint_sweep(carry, True)
 
     for copy in pending:
         copy.wait_send()
     for copy in decay_copies:
         copy.wait_send()
-    for d in range(1, SLABS):
-
-        @pl.when(tm + d < SLABS)
-        def _():
-            tm_copy(ends, 1, d).wait_send()
-            tm_copy(leaving, 2, d).wait_recv()
+    exchange(1, ends, ends_short, "wait_send")
+    exchange(2, leaving, leaving_short, "wait_recv")
 
     carry = jnp.zeros((PROBES, WIDTH), F32)
     for s in reversed(range(1, SLABS)):
-        carry = jnp.where(s > tm, decay_of(s) * carry + leaving[s], carry)
+        carry = jnp.where(s > tm, decay_of(s) * carry + arrived(s, leaving, leaving_short), carry)
 
     for n in range(8):
         cols = slice(n * 128, (n + 1) * 128)
@@ -522,11 +553,7 @@
             return c
 
         lax.fori_loop(0, DAYS // 8, finish, part_carry)
-    for d in range(1, SLABS):
-
-        @pl.when(tm - d >= 0)
-        def _():
-            tm_copy(leaving, 2, d).wait_send()
+    exchange(2, leaving, leaving_short, "wait_send")
 
 
 def local(
@@ -573,8 +600,11 @@
             pltpu.VMEM((DAYS, WIDTH), F32),
             pltpu.VMEM((DAYS, WIDTH), F32),
             pltpu.VMEM((SLABS, 8, 128), F32),
+            pltpu.VMEM((4, 256, 256), F32),
             pltpu.VMEM((SLABS, PROBES, WIDTH), F32),
+            pltpu.VMEM((SLABS, PROBES, WIDTH), BF16),
             pltpu.VMEM((SLABS, PROBES, WIDTH), F32),
+            pltpu.VMEM((SLABS, PROBES, WIDTH), BF16),
             pltpu.SemaphoreType.DMA((CHUNKS + 3,)),
             pltpu.SemaphoreType.DMA((CHUNKS * 20,)),
             pltpu.SemaphoreType.DMA((CHUNKS * 20,)),

time: 58.2 us -> 51 us (0.88)
  the two profiles are of different devices: /device:TPU:0 before, /device:TPU:1 now
where the time goes in v2:
time: 51 us; the launch traced here: 50.8 us
  Pallas kernels  48.6 us (95%)
  local copies, waits for them, and re-layouts  1.62 us (3%)
  between operations  0.66 us (1%)
    pallas_call x1, Pallas kernels, local(): pl.pallas_call(kernel, out_shape=jax.ShapeDtypeStruct((DAYS, WIDTH), F32)...  48.6 us
    unnamed x1, local copies, waits for them, and re-layouts  1.62 us

profile of v2, /device:TPU:1, one launch (start us, length us, event | category | flops | bytes accessed | tf_op | source)
XLA Modules:
  0.0 50.8 jit_solution(11768584884834246280)
XLA Ops:
  0.7 48.6 %shard_map.91 = f32[48,1024]{1,0:T(8,128)} custom-call(s32[4,16]{1,0:T(4,128)} %bitcast.4, s32[2,16]{1,0:T(2,128)} %bitcast.5, s32[1,2]{1,0:T(1,128)} %shared_blocks.1, s32[1]{0:T(128)S(6)} %copy.11.slab_days, bf16[768,1024]{1,0:T(8,128)(2,1)} %bitcast.3, bf16[16,4,64,64]{3,2,1,0:T(8,128)(2,1)} %local_hbm.1, bf16[16,2,64,64]{3,2,1,0:T(8,128)(2,1)} %remote_hbm.1, ...), custom_call_target="tpu_custom_call" | custom-call | tf_op jit(solution)/shard_map/pallas_call | solution.py:573
  49.2 1.6 %copy.12 = f32[48,1024]{1,0:T(8,128)} copy(f32[48,1024]{1,0:T(8,128)} %shard_map.91) | data formatting | bytes 393216

commit v3 on v2

--- a/solution.py
+++ b/solution.py
@@ -96,14 +96,17 @@
         pltpu.make_async_copy(remote_hbm, remote_w, in_sem.at[CHUNKS + 1]),
         pltpu.make_async_copy(inverse_hbm, inverse_w, in_sem.at[CHUNKS + 2]),
     ]
-    for copy in fetch + weights:
+    for copy in fetch:
         copy.start()
 
     def shuffle_rows(r, carry):
-        source = lax.broadcasted_iota(jnp.int32, (64, WIDTH), 0) + r * 64
-        target = lax.broadcasted_iota(jnp.int32, (64, WIDTH), 1)
-        hit = target == (source % PROBES) * BS + source // PROBES
-        shuffle[pl.ds(pl.multiple_of(r * 64, 64), 64), :] = jnp.where(hit, 1.0, 0.0).astype(BF16)
+        source = lax.broadcasted_iota(jnp.int32, (64, 128), 0) + r * 64
+        gap = (source & (PROBES - 1)) * BS + (source >> 4)
+        gap = gap - lax.broadcasted_iota(jnp.int32, (64, 128), 1)
+        for q in range(8):
+            shuffle[pl.ds(pl.multiple_of(r * 64, 64), 64), q * 128 : (q + 1) * 128] = jnp.where(
+                gap == q * 128, 1.0, 0.0
+            ).astype(BF16)
         return carry
 
     lax.fori_loop(0, WIDTH // 64, shuffle_rows, 0)
@@ -201,7 +204,7 @@
         return copy
 
     flows = [{} for _ in range(CHUNKS)]
-    across = [[] for _ in range(CHUNKS)]
+    across = {"near": [], "middle": [], "last": []}
     N = CHUNK_ROWS
 
     def send_own(k):
@@ -209,41 +212,44 @@
         f["y"] = send(me, k, 0, N, at(0, 1, 0))
         f["p0"] = send(me, k, 0, N, at(1, 0, 0))
         f["m0"] = send(me, k, 0, N, at(3, 0, 0))
-        across[k].append(send(me, k, 0, N, sibling))
+        across["near"].append(send(me, k, 0, N, sibling))
 
     def relay_first(k):
         f = flows[k]
         f["y"].wait_recv()
         f["p1"] = send(at(0, 1, 0), k, 0, N, at(1, 0, 0))
         f["m1"] = send(at(0, 1, 0), k, 0, N, at(3, 0, 0))
-        across[k].append(send(at(0, 1, 0), k, 0, N, sibling))
+        across["near"].append(send(at(0, 1, 0), k, 0, N, sibling))
         f["p0"].wait_recv()
         f["pp0"] = send(at(3, 0, 0), k, 0, HALF, at(1, 0, 0))
-        across[k].append(send(at(3, 0, 0), k, 0, N, sibling))
+        across["near"].append(send(at(3, 0, 0), k, 0, N, sibling))
         f["m0"].wait_recv()
         f["mm0"] = send(at(1, 0, 0), k, HALF, HALF, at(3, 0, 0))
-        across[k].append(send(at(1, 0, 0), k, 0, N, sibling))
+        across["near"].append(send(at(1, 0, 0), k, 0, N, sibling))
 
     def relay_second(k):
         f = flows[k]
         f["p1"].wait_recv()
         f["pp1"] = send(at(3, 1, 0), k, 0, HALF, at(1, 0, 0))
-        across[k].append(send(at(3, 1, 0), k, 0, N, sibling))
+        across["middle"].append(send(at(3, 1, 0), k, 0, N, sibling))
         f["m1"].wait_recv()
         f["mm1"] = send(at(1, 1, 0), k, HALF, HALF, at(3, 0, 0))
-        across[k].append(send(at(1, 1, 0), k, 0, N, sibling))
+        across["middle"].append(send(at(1, 1, 0), k, 0, N, sibling))
 
     def relay_third(k):
         f = flows[k]
         f["pp0"].wait_recv()
         f["mm0"].wait_recv()
-        across[k].append(send(at(2, 0, 0), k, 0, N, sibling))
+        across["middle"].append(send(at(2, 0, 0), k, 0, N, sibling))
+
+    def relay_fourth(k):
+        f = flows[k]
         f["pp1"].wait_recv()
         f["mm1"].wait_recv()
-        across[k].append(send(at(2, 1, 0), k, 0, N, sibling))
-
-    def all_here(k):
-        for copy in across[k]:
+        across["last"].append(send(at(2, 1, 0), k, 0, N, sibling))
+
+    def all_here(stage):
+        for copy in across[stage]:
             copy.wait_recv()
 
     def turn(weight, degree, first):
@@ -291,9 +297,9 @@
                 lane = place // 2 * 128
                 out[quad, place * BS : (place + 1) * BS, lane : lane + 128] = wide.astype(BF16)
 
-    def couple_local(k):
+    def couple_local():
         def part(r, carry):
-            rows = pl.ds(pl.multiple_of(k * CHUNK_ROWS + r * SUB, SUB), SUB)
+            rows = pl.ds(pl.multiple_of(r * SUB, SUB), SUB)
             for n in range(4):
                 cols = slice(n * 256, (n + 1) * 256)
                 total[rows, cols] = total[rows, cols] - jnp.dot(
@@ -301,18 +307,33 @@
                 )
             return carry
 
-        lax.fori_loop(0, CHUNK_ROWS // SUB, part, 0)
-
-    def couple_remote(k):
+        lax.fori_loop(0, ROWS // SUB, part, 0)
+
+    def couple_remote(*chips):
+        places = [at(dx, dy, 0) // 2 for dx, dy in chips]
+
         def part(r, carry):
-            rows = pl.ds(pl.multiple_of(k * CHUNK_ROWS + r * SUB, SUB), SUB)
-            inner = pl.ds(pl.multiple_of(r * SUB, SUB), SUB)
+            rows = pl.ds(pl.multiple_of(r * SUB, SUB), SUB)
+            k = r // (CHUNK_ROWS // SUB)
+            inner = pl.ds(pl.multiple_of(r % (CHUNK_ROWS // SUB) * SUB, SUB), SUB)
             for n in range(4):
                 cols = slice(n * 256, (n + 1) * 256)
-                left = jnp.concatenate([shared[k, g, inner, :] for g in range(GROUPS)], axis=1)
+                left = jnp.concatenate(
+                    [shared[k, 2 * q + c, inner, :] for q in places for c in range(2)], axis=1
+                )
+                right = jnp.concatenate(
+                    [far[pl.ds(pl.multiple_of(q * 256, 256), 256), cols] for q in places], axis=0
+                )
                 total[rows, cols] = total[rows, cols] - jnp.dot(
-                    left, far[:, cols], preferred_element_type=F32
+                    left, right, preferred_element_type=F32
                 )
+            return carry
+
+        lax.fori_loop(0, ROWS // SUB, part, 0)
+
+    def force():
+        def part(r, carry):
+            rows = pl.ds(pl.multiple_of(r * SUB, SUB), SUB)
             for n in range(4):
                 cols = slice(n * 256, (n + 1) * 256)
                 states[rows, cols] = jnp.dot(
@@ -320,7 +341,7 @@
                 )
             return carry
 
-        lax.fori_loop(0, CHUNK_ROWS // SUB, part, 0)
+        lax.fori_loop(0, ROWS // SUB, part, 0)
 
     def scan_forward(k, state):
         def day(t, s):
@@ -353,13 +374,12 @@
         for q in range(8):
             slab_decay[tm, q : q + 1, :] = product[:, q * 128 : (q + 1) * 128]
 
-    def tm_copy(buf, kind, d):
-        to = (tm + d) % SLABS if kind < 2 else (tm + SLABS - d) % SLABS
+    def tm_copy(buf, to, send, recv):
         return pltpu.make_async_remote_copy(
             src_ref=buf.at[tm],
             dst_ref=buf.at[tm],
-            send_sem=tm_send.at[kind * 8 + d],
-            recv_sem=tm_recv.at[kind * 8 + d],
+            send_sem=tm_send.at[send],
+            recv_sem=tm_recv.at[recv],
             device_id=(to, space),
             device_id_type=MESH,
         )
@@ -368,19 +388,22 @@
         return other // (SLABS // 2) == tm // (SLABS // 2)
 
     def exchange(kind, wide, narrow, act):
-        for d in range(1, SLABS):
+        for d in reversed(range(1, SLABS)):
             ahead = (kind == 1) == (act != "wait_recv")
             other = tm + d if ahead else tm - d
             real = other < SLABS if ahead else other >= 0
             near_by = same_row(other)
 
+            peer = (other + SLABS) % SLABS
+            signal = peer if act == "wait_recv" else tm
+
             @pl.when(jnp.logical_and(real, near_by))
             def _():
-                getattr(tm_copy(wide, kind, d), act)()
+                getattr(tm_copy(wide, peer, peer, signal), act)()
 
             @pl.when(jnp.logical_and(real, jnp.logical_not(near_by)))
             def _():
-                getattr(tm_copy(narrow, kind, d), act)()
+                getattr(tm_copy(narrow, peer, peer, signal), act)()
 
     def arrived(s, wide, narrow):
         return jnp.where(same_row(s), wide[s], narrow[s].astype(F32))
@@ -404,39 +427,48 @@
     for k in range(CHUNKS):
         fetch[k].wait()
     pick_shared()
-    prepare_decay()
+    for copy in weights:
+        copy.start()
     pl.semaphore_wait(barrier, 4 + SLABS - 1)
     for k in range(CHUNKS):
         send_own(k)
-    decay_copies = [tm_copy(slab_decay, 0, d) for d in range(1, SLABS)]
+    prepare_decay()
+    decay_copies = [
+        tm_copy(slab_decay, (tm + d) % SLABS, SLABS + d - 1, SLABS + d - 1)
+        for d in range(1, SLABS)
+    ]
     for copy in decay_copies:
         copy.start()
     permute(0)
     permute(1)
-    relay_first(0)
     order(0)
-    relay_first(1)
     order(1)
     weights[0].wait()
+    weights[1].wait()
     turn(local_w, 4, 0)
+    turn(remote_w, 2, 4)
+    relay_first(0)
+    relay_first(1)
     build(local_links, BLOCKS, 4, 0, near)
+    build(remote_links, 2 * GROUPS, 2, 4, far)
+    couple_local()
     relay_second(0)
-    weights[1].wait()
-    turn(remote_w, 2, 4)
-    build(remote_links, 2 * GROUPS, 2, 4, far)
     relay_second(1)
-    couple_local(0)
+    all_here("near")
+    couple_remote((0, 0), (1, 0), (3, 0), (0, 1))
     relay_third(0)
-    couple_local(1)
+    relay_third(1)
     weights[2].wait()
     build_inverse()
     prepare_response()
-    all_here(0)
-    couple_remote(0)
+    all_here("middle")
+    couple_remote((2, 0), (1, 1), (3, 1))
+    relay_fourth(0)
+    relay_fourth(1)
+    all_here("last")
+    couple_remote((2, 1))
+    force()
     state = scan_forward(0, jnp.zeros((PROBES, WIDTH), F32))
-    relay_third(1)
-    all_here(1)
-    couple_remote(1)
     state = scan_forward(1, state)
     ends[tm] = state
     ends_short[tm] = state.astype(BF16)
@@ -606,10 +638,10 @@
             pltpu.VMEM((SLABS, PROBES, WIDTH), F32),
             pltpu.VMEM((SLABS, PROBES, WIDTH), BF16),
             pltpu.SemaphoreType.DMA((CHUNKS + 3,)),
-            pltpu.SemaphoreType.DMA((CHUNKS * 20,)),
-            pltpu.SemaphoreType.DMA((CHUNKS * 20,)),
-            pltpu.SemaphoreType.DMA((24,)),
-            pltpu.SemaphoreType.DMA((24,)),
+            pltpu.SemaphoreType.DMA((CHUNKS * 17,)),
+            pltpu.SemaphoreType.DMA((CHUNKS * 17,)),
+            pltpu.SemaphoreType.DMA((2 * SLABS - 1,)),
+            pltpu.SemaphoreType.DMA((2 * SLABS - 1,)),
         ],
         compiler_params=pltpu.CompilerParams(
             vmem_limit_bytes=60 << 20, collective_id=0, has_side_effects=True

time: 51 us -> 48.3 us (0.947)
  the two profiles are of different devices: /device:TPU:1 before, /device:TPU:0 now
where the time goes in v3:
time: 48.3 us; the launch traced here: 47.6 us
  Pallas kernels  45.3 us (94%)
  local copies, waits for them, and re-layouts  1.62 us (3%)
  between operations  0.66 us (1%)
    pallas_call x1, Pallas kernels, local(): pl.pallas_call(kernel, out_shape=jax.ShapeDtypeStruct((DAYS, WIDTH), F32)...  45.3 us
    unnamed x1, local copies, waits for them, and re-layouts  1.62 us

profile of v3, /device:TPU:0, one launch (start us, length us, event | category | flops | bytes accessed | tf_op | source)
XLA Modules:
  0.0 47.6 jit_solution(3489550982968821108)
XLA Ops:
  0.7 45.3 %shard_map.91 = f32[48,1024]{1,0:T(8,128)} custom-call(s32[4,16]{1,0:T(4,128)} %bitcast.4, s32[2,16]{1,0:T(2,128)} %bitcast.5, s32[1,2]{1,0:T(1,128)} %shared_blocks.1, s32[1]{0:T(128)S(6)} %copy.11.slab_days, bf16[768,1024]{1,0:T(8,128)(2,1)} %bitcast.3, bf16[16,4,64,64]{3,2,1,0:T(8,128)(2,1)} %local_hbm.1, bf16[16,2,64,64]{3,2,1,0:T(8,128)(2,1)} %remote_hbm.1, ...), custom_call_target="tpu_custom_call" | custom-call | tf_op jit(solution)/shard_map/pallas_call | solution.py:605
  45.9 1.6 %copy.12 = f32[48,1024]{1,0:T(8,128)} copy(f32[48,1024]{1,0:T(8,128)} %shard_map.91) | data formatting | bytes 393216

commit v4 on v3

--- a/solution.py
+++ b/solution.py
@@ -60,9 +60,7 @@
     slab_decay,
     response,
     ends,
-    ends_short,
     leaving,
-    leaving_short,
     in_sem,
     send_sem,
     recv_sem,
@@ -220,6 +218,9 @@
         f["p1"] = send(at(0, 1, 0), k, 0, N, at(1, 0, 0))
         f["m1"] = send(at(0, 1, 0), k, 0, N, at(3, 0, 0))
         across["near"].append(send(at(0, 1, 0), k, 0, N, sibling))
+
+    def relay_own_row(k):
+        f = flows[k]
         f["p0"].wait_recv()
         f["pp0"] = send(at(3, 0, 0), k, 0, HALF, at(1, 0, 0))
         across["near"].append(send(at(3, 0, 0), k, 0, N, sibling))
@@ -309,7 +310,7 @@
 
         lax.fori_loop(0, ROWS // SUB, part, 0)
 
-    def couple_remote(*chips):
+    def couple_remote(*chips, rows_of=range(CHUNKS)):
         places = [at(dx, dy, 0) // 2 for dx, dy in chips]
 
         def part(r, carry):
@@ -329,9 +330,10 @@
                 )
             return carry
 
-        lax.fori_loop(0, ROWS // SUB, part, 0)
-
-    def force():
+        steps = CHUNK_ROWS // SUB
+        lax.fori_loop(rows_of[0] * steps, (rows_of[-1] + 1) * steps, part, 0)
+
+    def force(k):
         def part(r, carry):
             rows = pl.ds(pl.multiple_of(r * SUB, SUB), SUB)
             for n in range(4):
@@ -341,7 +343,7 @@
                 )
             return carry
 
-        lax.fori_loop(0, ROWS // SUB, part, 0)
+        lax.fori_loop(k * (CHUNK_ROWS // SUB), (k + 1) * (CHUNK_ROWS // SUB), part, 0)
 
     def scan_forward(k, state):
         def day(t, s):
@@ -384,29 +386,17 @@
             device_id_type=MESH,
         )
 
-    def same_row(other):
-        return other // (SLABS // 2) == tm // (SLABS // 2)
-
-    def exchange(kind, wide, narrow, act):
+    def exchange(kind, buf, act):
         for d in reversed(range(1, SLABS)):
             ahead = (kind == 1) == (act != "wait_recv")
             other = tm + d if ahead else tm - d
             real = other < SLABS if ahead else other >= 0
-            near_by = same_row(other)
-
             peer = (other + SLABS) % SLABS
             signal = peer if act == "wait_recv" else tm
 
-            @pl.when(jnp.logical_and(real, near_by))
+            @pl.when(real)
             def _():
-                getattr(tm_copy(wide, peer, peer, signal), act)()
-
-            @pl.when(jnp.logical_and(real, jnp.logical_not(near_by)))
-            def _():
-                getattr(tm_copy(narrow, peer, peer, signal), act)()
-
-    def arrived(s, wide, narrow):
-        return jnp.where(same_row(s), wide[s], narrow[s].astype(F32))
+                getattr(tm_copy(buf, peer, peer, signal), act)()
 
     def prepare_response():
         for n in range(4):
@@ -448,9 +438,11 @@
     turn(local_w, 4, 0)
     turn(remote_w, 2, 4)
     relay_first(0)
+    relay_own_row(0)
     relay_first(1)
     build(local_links, BLOCKS, 4, 0, near)
     build(remote_links, 2 * GROUPS, 2, 4, far)
+    relay_own_row(1)
     couple_local()
     relay_second(0)
     relay_second(1)
@@ -465,14 +457,14 @@
     couple_remote((2, 0), (1, 1), (3, 1))
     relay_fourth(0)
     relay_fourth(1)
-    all_here("last")
-    couple_remote((2, 1))
-    force()
-    state = scan_forward(0, jnp.zeros((PROBES, WIDTH), F32))
-    state = scan_forward(1, state)
-    ends[tm] = state
-    ends_short[tm] = state.astype(BF16)
-    exchange(1, ends, ends_short, "start")
+    state = jnp.zeros((PROBES, WIDTH), F32)
+    for k in range(CHUNKS):
+        across["last"][k].wait_recv()
+        couple_remote((2, 1), rows_of=[k])
+        force(k)
+        state = scan_forward(k, state)
+    ends[tm] = state.astype(BF16)
+    exchange(1, ends, "start")
 
     row8 = lax.broadcasted_iota(jnp.int32, (8, 128), 0)
 
@@ -538,10 +530,10 @@
     leave = adjoint_sweep(0, False)
     for copy in decay_copies:
         copy.wait_recv()
-    exchange(1, ends, ends_short, "wait_recv")
+    exchange(1, ends, "wait_recv")
     carry = jnp.zeros((PROBES, WIDTH), F32)
     for s in range(SLABS - 1):
-        carry = jnp.where(s < tm, decay_of(s) * carry + arrived(s, ends, ends_short), carry)
+        carry = jnp.where(s < tm, decay_of(s) * carry + ends[s].astype(F32), carry)
     for n in range(4):
         cols = slice(n * 256, (n + 1) * 256)
         value = leave[n] + jnp.dot(
@@ -550,42 +542,40 @@
             precision=lax.Precision.HIGHEST,
             preferred_element_type=F32,
         )
-        leaving[tm, :, cols] = value
-        leaving_short[tm, :, cols] = value.astype(BF16)
-    exchange(2, leaving, leaving_short, "start")
+        leaving[tm, :, cols] = value.astype(BF16)
+    exchange(2, leaving, "start")
     adjoint_sweep(carry, True)
 
     for copy in pending:
         copy.wait_send()
     for copy in decay_copies:
         copy.wait_send()
-    exchange(1, ends, ends_short, "wait_send")
-    exchange(2, leaving, leaving_short, "wait_recv")
+    exchange(1, ends, "wait_send")
+    exchange(2, leaving, "wait_recv")
 
     carry = jnp.zeros((PROBES, WIDTH), F32)
     for s in reversed(range(1, SLABS)):
-        carry = jnp.where(s > tm, decay_of(s) * carry + arrived(s, leaving, leaving_short), carry)
-
-    for n in range(8):
-        cols = slice(n * 128, (n + 1) * 128)
-        part_carry = carry[:, cols]
-
-        def finish(g, c):
-            eight = pl.ds(pl.multiple_of(g * 8, 8), 8)
+        carry = jnp.where(s > tm, decay_of(s) * carry + leaving[s].astype(F32), carry)
+
+    def finish(g, c):
+        eight = pl.ds(pl.multiple_of(g * 8, 8), 8)
+        for n in range(8):
+            cols = slice(n * 128, (n + 1) * 128)
+            top, bottom = c[0:8, cols], c[8:16, cols]
             z = ordered[pl.ds(pl.multiple_of(g * 128, 128), 128), cols].astype(F32)
             extra = fold(
                 [
-                    z[16 * d : 16 * d + 8] * c[0:8] + z[16 * d + 8 : 16 * d + 16] * c[8:16]
+                    z[16 * d : 16 * d + 8] * top + z[16 * d + 8 : 16 * d + 16] * bottom
                     for d in range(8)
                 ]
             )
             out_ref[eight, cols] = (partial[eight, cols] + backward_decay[eight, cols] * extra) * (
                 1.0 / PROBES
             )
-            return c
-
-        lax.fori_loop(0, DAYS // 8, finish, part_carry)
-    exchange(2, leaving, leaving_short, "wait_send")
+        return c
+
+    lax.fori_loop(0, DAYS // 8, finish, carry)
+    exchange(2, leaving, "wait_send")
 
 
 def local(
@@ -633,9 +623,7 @@
             pltpu.VMEM((DAYS, WIDTH), F32),
             pltpu.VMEM((SLABS, 8, 128), F32),
             pltpu.VMEM((4, 256, 256), F32),
-            pltpu.VMEM((SLABS, PROBES, WIDTH), F32),
             pltpu.VMEM((SLABS, PROBES, WIDTH), BF16),
-            pltpu.VMEM((SLABS, PROBES, WIDTH), F32),
             pltpu.VMEM((SLABS, PROBES, WIDTH), BF16),
             pltpu.SemaphoreType.DMA((CHUNKS + 3,)),
             pltpu.SemaphoreType.DMA((CHUNKS * 17,)),

time: 48.3 us -> 45.6 us (0.944); the launches traced: 47.6 us -> 45.4 us
  Pallas kernels: 45.3 us -> 43.2 us
    pallas_call x1, Pallas kernels: 45.3 us -> 43.2 us  [local(): pl.pallas_call(kernel, out_shape=jax.ShapeDtypeStruct((DAYS, WIDTH), F32)...]
where the time goes in v4:
time: 45.6 us; the launch traced here: 45.4 us
  Pallas kernels  43.2 us (95%)
  local copies, waits for them, and re-layouts  1.62 us (4%)
  between operations  0.66 us (1%)
    pallas_call x1, Pallas kernels, local(): pl.pallas_call(kernel, out_shape=jax.ShapeDtypeStruct((DAYS, WIDTH), F32)...  43.2 us
    unnamed x1, local copies, waits for them, and re-layouts  1.62 us

profile of v4, /device:TPU:0, one launch (start us, length us, event | category | flops | bytes accessed | tf_op | source)
XLA Modules:
  0.0 45.4 jit_solution(9555789604705265739)
XLA Ops:
  0.7 43.2 %shard_map.91 = f32[48,1024]{1,0:T(8,128)} custom-call(s32[4,16]{1,0:T(4,128)} %bitcast.4, s32[2,16]{1,0:T(2,128)} %bitcast.5, s32[1,2]{1,0:T(1,128)} %shared_blocks.1, s32[1]{0:T(128)S(6)} %copy.11.slab_days, bf16[768,1024]{1,0:T(8,128)(2,1)} %bitcast.3, bf16[16,4,64,64]{3,2,1,0:T(8,128)(2,1)} %local_hbm.1, bf16[16,2,64,64]{3,2,1,0:T(8,128)(2,1)} %remote_hbm.1, ...), custom_call_target="tpu_custom_call" | custom-call | tf_op jit(solution)/shard_map/pallas_call | solution.py:595
  43.8 1.6 %copy.12 = f32[48,1024]{1,0:T(8,128)} copy(f32[48,1024]{1,0:T(8,128)} %shard_map.91) | data formatting | bytes 393216

commit v5 on v4

--- a/solution.py
+++ b/solution.py
@@ -215,33 +215,37 @@
     def relay_first(k):
         f = flows[k]
         f["y"].wait_recv()
-        f["p1"] = send(at(0, 1, 0), k, 0, N, at(1, 0, 0))
-        f["m1"] = send(at(0, 1, 0), k, 0, N, at(3, 0, 0))
+        f["p1"] = send(at(0, 1, 0), k, 0, HALF, at(1, 0, 0))
+        f["m1"] = send(at(0, 1, 0), k, HALF, HALF, at(3, 0, 0))
         across["near"].append(send(at(0, 1, 0), k, 0, N, sibling))
 
     def relay_own_row(k):
         f = flows[k]
         f["p0"].wait_recv()
         f["pp0"] = send(at(3, 0, 0), k, 0, HALF, at(1, 0, 0))
+        f["yp"] = send(at(3, 0, 0), k, HALF, HALF, at(0, 1, 0))
         across["near"].append(send(at(3, 0, 0), k, 0, N, sibling))
         f["m0"].wait_recv()
         f["mm0"] = send(at(1, 0, 0), k, HALF, HALF, at(3, 0, 0))
+        f["ym"] = send(at(1, 0, 0), k, 0, HALF, at(0, 1, 0))
         across["near"].append(send(at(1, 0, 0), k, 0, N, sibling))
 
     def relay_second(k):
         f = flows[k]
         f["p1"].wait_recv()
         f["pp1"] = send(at(3, 1, 0), k, 0, HALF, at(1, 0, 0))
-        across["middle"].append(send(at(3, 1, 0), k, 0, N, sibling))
         f["m1"].wait_recv()
         f["mm1"] = send(at(1, 1, 0), k, HALF, HALF, at(3, 0, 0))
-        across["middle"].append(send(at(1, 1, 0), k, 0, N, sibling))
 
     def relay_third(k):
         f = flows[k]
         f["pp0"].wait_recv()
         f["mm0"].wait_recv()
         across["middle"].append(send(at(2, 0, 0), k, 0, N, sibling))
+        f["yp"].wait_recv()
+        across["middle"].append(send(at(3, 1, 0), k, 0, N, sibling))
+        f["ym"].wait_recv()
+        across["middle"].append(send(at(1, 1, 0), k, 0, N, sibling))
 
     def relay_fourth(k):
         f = flows[k]
@@ -298,7 +302,7 @@
                 lane = place // 2 * 128
                 out[quad, place * BS : (place + 1) * BS, lane : lane + 128] = wide.astype(BF16)
 
-    def couple_local():
+    def couple_local(k):
         def part(r, carry):
             rows = pl.ds(pl.multiple_of(r * SUB, SUB), SUB)
             for n in range(4):
@@ -308,7 +312,7 @@
                 )
             return carry
 
-        lax.fori_loop(0, ROWS // SUB, part, 0)
+        lax.fori_loop(k * (CHUNK_ROWS // SUB), (k + 1) * (CHUNK_ROWS // SUB), part, 0)
 
     def couple_remote(*chips, rows_of=range(CHUNKS)):
         places = [at(dx, dy, 0) // 2 for dx, dy in chips]
@@ -440,11 +444,12 @@
     relay_first(0)
     relay_own_row(0)
     relay_first(1)
+    relay_own_row(1)
     build(local_links, BLOCKS, 4, 0, near)
     build(remote_links, 2 * GROUPS, 2, 4, far)
-    relay_own_row(1)
-    couple_local()
+    couple_local(0)
     relay_second(0)
+    couple_local(1)
     relay_second(1)
     all_here("near")
     couple_remote((0, 0), (1, 0), (3, 0), (0, 1))
@@ -626,8 +631,8 @@
             pltpu.VMEM((SLABS, PROBES, WIDTH), BF16),
             pltpu.VMEM((SLABS, PROBES, WIDTH), BF16),
             pltpu.SemaphoreType.DMA((CHUNKS + 3,)),
-            pltpu.SemaphoreType.DMA((CHUNKS * 17,)),
-            pltpu.SemaphoreType.DMA((CHUNKS * 17,)),
+            pltpu.SemaphoreType.DMA((CHUNKS * 19,)),
+            pltpu.SemaphoreType.DMA((CHUNKS * 19,)),
             pltpu.SemaphoreType.DMA((2 * SLABS - 1,)),
             pltpu.SemaphoreType.DMA((2 * SLABS - 1,)),
         ],

time: 45.6 us -> 44.9 us (0.985)
  Pallas kernels: 43.2 us -> 42.4 us
    pallas_call x1, Pallas kernels: 43.2 us -> 42.4 us  [local(): pl.pallas_call(kernel, out_shape=jax.ShapeDtypeStruct((DAYS, WIDTH), F32)...]
where the time goes in v5:
time: 44.9 us; the launch traced here: 44.7 us
  Pallas kernels  42.4 us (94%)
  local copies, waits for them, and re-layouts  1.62 us (4%)
  between operations  0.66 us (1%)
    pallas_call x1, Pallas kernels, local(): pl.pallas_call(kernel, out_shape=jax.ShapeDtypeStruct((DAYS, WIDTH), F32)...  42.4 us
    unnamed x1, local copies, waits for them, and re-layouts  1.62 us

profile of v5, /device:TPU:0, one launch (start us, length us, event | category | flops | bytes accessed | tf_op | source)
XLA Modules:
  0.0 44.7 jit_solution(2364369290401954087)
XLA Ops:
  0.7 42.4 %shard_map.91 = f32[48,1024]{1,0:T(8,128)} custom-call(s32[4,16]{1,0:T(4,128)} %bitcast.4, s32[2,16]{1,0:T(2,128)} %bitcast.5, s32[1,2]{1,0:T(1,128)} %shared_blocks.1, s32[1]{0:T(128)S(6)} %copy.11.slab_days, bf16[768,1024]{1,0:T(8,128)(2,1)} %bitcast.3, bf16[16,4,64,64]{3,2,1,0:T(8,128)(2,1)} %local_hbm.1, bf16[16,2,64,64]{3,2,1,0:T(8,128)(2,1)} %remote_hbm.1, ...), custom_call_target="tpu_custom_call" | custom-call | tf_op jit(solution)/shard_map/pallas_call | solution.py:600
  43.1 1.6 %copy.12 = f32[48,1024]{1,0:T(8,128)} copy(f32[48,1024]{1,0:T(8,128)} %shard_map.91) | data formatting | bytes 393216

commit v6 on v5

--- a/solution.py
+++ b/solution.py
@@ -441,6 +441,9 @@
     weights[1].wait()
     turn(local_w, 4, 0)
     turn(remote_w, 2, 4)
+    weights[2].wait()
+    build_inverse()
+    prepare_response()
     relay_first(0)
     relay_own_row(0)
     relay_first(1)
@@ -455,9 +458,6 @@
     couple_remote((0, 0), (1, 0), (3, 0), (0, 1))
     relay_third(0)
     relay_third(1)
-    weights[2].wait()
-    build_inverse()
-    prepare_response()
     all_here("middle")
     couple_remote((2, 0), (1, 1), (3, 1))
     relay_fourth(0)

time: 44.9 us -> 44.5 us (level)
  no operation moved by 1% of the time
where the time goes in v6:
time: 44.5 us; the launch traced here: 44.4 us
  Pallas kernels  42.1 us (95%)
  local copies, waits for them, and re-layouts  1.62 us (4%)
  between operations  0.66 us (1%)
    pallas_call x1, Pallas kernels, local(): pl.pallas_call(kernel, out_shape=jax.ShapeDtypeStruct((DAYS, WIDTH), F32)...  42.1 us
    unnamed x1, local copies, waits for them, and re-layouts  1.62 us

profile of v6, /device:TPU:0, one launch (start us, length us, event | category | flops | bytes accessed | tf_op | source)
XLA Modules:
  0.0 44.4 jit_solution(1791227288576645860)
XLA Ops:
  0.7 42.1 %shard_map.91 = f32[48,1024]{1,0:T(8,128)} custom-call(s32[4,16]{1,0:T(4,128)} %bitcast.4, s32[2,16]{1,0:T(2,128)} %bitcast.5, s32[1,2]{1,0:T(1,128)} %shared_blocks.1, s32[1]{0:T(128)S(6)} %copy.11.slab_days, bf16[768,1024]{1,0:T(8,128)(2,1)} %bitcast.3, bf16[16,4,64,64]{3,2,1,0:T(8,128)(2,1)} %local_hbm.1, bf16[16,2,64,64]{3,2,1,0:T(8,128)(2,1)} %remote_hbm.1, ...), custom_call_target="tpu_custom_call" | custom-call | tf_op jit(solution)/shard_map/pallas_call | solution.py:600
  42.7 1.6 %copy.12 = f32[48,1024]{1,0:T(8,128)} copy(f32[48,1024]{1,0:T(8,128)} %shard_map.91) | data formatting | bytes 393216
